TPU v7x, 256 devices: a whole 4x4x8 slice. The times are simulated.
256 devices in a mesh: dp: 32 (over z, x), tensor: 8 (over y, core).
Axes of the slice: x: 4, y: 4, z: 8, core: 2. Of those that a mesh axis runs over, the one named last changes fastest.
Arguments:
- queries: bfloat16 [20480, 4096], P('dp', 'tensor'), may hold values from -6 to 6
- resp_kv: bfloat16 [20480, 2048], P('dp', 'tensor'), may hold values from -6 to 6
- prompt_kv: bfloat16 [512, 512, 2048], P('dp', None, 'tensor'), may hold values from -6 to 6
- prompt_len: int32 [512], replicated, may hold values from 128 to 512
- resp_len: int32 [512, 5], P('dp'), may hold values from 1 to 8
- dest: int32 [512], replicated, may hold values from 0 to 511, as said below
- wo: bfloat16 [4096, 8192], P('tensor'), may hold values from -0.09375 to 0.09375
- residual: bfloat16 [20480, 8192], P(('dp', 'tensor')), may hold values from -6 to 6
Outputs:
- hidden: bfloat16 [20480, 8192], P(('dp', 'tensor'))
Inputs may be any that keep to these rules, and one draw needn't show every extreme that they name: dest is a permutation; the 16 prompts prefilled on one dp index go to 16 different dp indices (slot // 16), so every dp index receives exactly 16 prompts, from different indices.
All inputs are finite; a program needn't handle non-finite values.
Results may differ from a plain program's by a relative error of at most 0.007.
Values may be sent and summed in bfloat16 or wider, within the bound.
A program may use at most 128 MiB of HBM per device.

v0:
```python
import jax
import jax.numpy as jnp
from jax import lax
from jax.sharding import PartitionSpec as P

HD = 128
RESP = 5


def attend(query, own, blocks, live, rlen_size):
    count = query.shape[0]
    heads = query.shape[3] * query.shape[4]
    scale = HD ** (-0.5)
    plen_size = blocks.shape[1]
    score_p = (
        jnp.einsum(
            "jrthgd,jshd->jrthgs", query, blocks[:, :, :, 0], preferred_element_type=jnp.float32
        )
        * scale
    )
    score_r = (
        jnp.einsum(
            "jrthgd,jruhd->jrthgu", query, own[:, :, :, :, 0], preferred_element_type=jnp.float32
        )
        * scale
    )
    pmask = (jnp.arange(plen_size)[None, :] < live[:, None])[:, None, None, None, None, :]
    causal = (jnp.arange(rlen_size)[:, None] >= jnp.arange(rlen_size)[None, :])[
        None, None, :, None, None, :
    ]
    score_p = jnp.where(pmask, score_p, -1e30)
    score_r = jnp.where(causal, score_r, -1e30)
    top = jnp.maximum(jnp.max(score_p, axis=-1), jnp.max(score_r, axis=-1))[..., None]
    exp_p = jnp.exp(score_p - top)
    exp_r = jnp.exp(score_r - top)
    denom = jnp.sum(exp_p, axis=-1, keepdims=True) + jnp.sum(exp_r, axis=-1, keepdims=True)
    weight_p = (exp_p / denom).astype(jnp.bfloat16)
    weight_r = (exp_r / denom).astype(jnp.bfloat16)
    out = jnp.einsum(
        "jrthgs,jshd->jrthgd", weight_p, blocks[:, :, :, 1], preferred_element_type=jnp.float32
    )
    out = out + jnp.einsum(
        "jrthgu,jruhd->jrthgd", weight_r, own[:, :, :, :, 1], preferred_element_type=jnp.float32
    )
    return out.reshape(count, RESP, rlen_size, heads * HD).astype(jnp.bfloat16)


def per_device(queries, resp_kv, prompt_kv, prompt_len, resp_len, dest, wo, residual):
    ndevices = lax.axis_size("dp")
    myself = lax.axis_index("dp")
    pdev, plen_size, kvwidth = prompt_kv.shape
    kvheads = kvwidth // (2 * HD)
    qwidth = queries.shape[1]
    heads = qwidth // HD
    group = heads // kvheads
    total = dest.shape[0]
    span = queries.shape[0] // pdev
    rlen_size = span // RESP
    inverse = jnp.zeros((total,), jnp.int32).at[dest].set(jnp.arange(total, dtype=jnp.int32))
    local_index = myself * pdev + jnp.arange(pdev, dtype=jnp.int32)
    chosen = inverse[local_index]
    prompt_home = chosen // pdev
    score_home = dest[local_index] // pdev
    outgoing = jnp.zeros((ndevices, plen_size, kvwidth), jnp.bfloat16).at[score_home].set(prompt_kv)
    incoming = lax.all_to_all(outgoing, "dp", split_axis=0, concat_axis=0, tiled=True)
    blocks = jnp.take(incoming, prompt_home, axis=0).reshape(pdev, plen_size, kvheads, 2, HD)
    live = prompt_len[chosen]
    query = queries.reshape(pdev, RESP, rlen_size, kvheads, group, HD)
    own = resp_kv.reshape(pdev, RESP, rlen_size, kvheads, 2, HD)
    attended = attend(query, own, blocks, live, rlen_size)
    valid = jnp.arange(rlen_size)[None, None, :] < resp_len[:, :, None]
    attended = jnp.where(valid[..., None], attended, jnp.zeros((), jnp.bfloat16))
    attended = attended.reshape(pdev * span, qwidth)
    partial_sum = jnp.dot(attended, wo, preferred_element_type=jnp.float32)
    mixed = lax.psum_scatter(
        partial_sum.astype(jnp.bfloat16), "tensor", scatter_dimension=0, tiled=True
    ).astype(jnp.float32)
    return (mixed + residual.astype(jnp.float32)).astype(jnp.bfloat16)


def solution(mesh):
    in_specs = (
        P("dp", "tensor"),
        P("dp", "tensor"),
        P("dp", None, "tensor"),
        P(),
        P("dp", None),
        P(),
        P("tensor", None),
        P(("dp", "tensor"), None),
    )
    out_specs = P(("dp", "tensor"), None)
    return jax.shard_map(
        per_device, mesh=mesh, in_specs=in_specs, out_specs=out_specs, check_vma=False
    )
```

profile of v0, /device:TPU:2, one launch (start us, length us, event | category | flops | bytes accessed | tf_op | source)
XLA Modules:
  0.0 341.4 jit_solution(14656413813843633720)
XLA Ops:
  6.5 0.0 copy-start
  6.6 1.4 gather_fusion.1
  8.0 4.2 %broadcast_in_dim.71 = bf16[32,512,256]{2,1,0:T(8,128)(2,1)} broadcast(bf16[]{:T(256)} %constant.57.clone.1), dimensions={} | broadcast | bytes 8388610 | tf_op jit(solution)/shard_map/broadcast_in_dim | solution.py:64
  12.1 11.0 %scatter_fusion = bf16[32,512,256]{2,1,0:T(8,128)(2,1)} fusion(bf16[32,512,256]{2,1,0:T(8,128)(2,1)} %broadcast_in_dim.71, s32[16]{0:T(128)S(1)} %fusion.27, bf16[16,512,256]{2,1,0:T(8,128)(2,1)} %param.10), kind=kCustom, calls=%fused_computation.5 | custom fusion | bytes 12582976 | tf_op jit(solution)/shard_map/scatter | solution.py:64
  23.1 11.8 %all-to-all-start = ((bf16[32,512,256]{2,1,0:T(8,128)(2,1)}), bf16[32,512,256]{2,1,0:T(8,128)(2,1)}, u32[]{:S(2)}, u32[]{:S(2)}) async-start(bf16[32,512,256]{2,1,0:T(8,128)(2,1)} %scatter_fusion), calls=%async_computation | async-start | bytes 16777216 | tf_op jit(solution)/shard_map/all_to_all | solution.py:65
  34.9 0.0 reduce-scatter.2.cloned.1.call-start
  35.0 0.0 copy-done.2
  35.0 2.6 scatter_custom_fusion
  37.7 0.7 gather_fusion
  38.3 0.1 copy.11
  38.4 0.1 iota_compare_fusion
  38.5 0.1 lt.81
  38.6 0.7 gather_fusion.3
  39.3 0.1 iota_compare_fusion.1
  39.4 3.0 fusion.32
  42.4 182.2 %all-to-all-done = bf16[32,512,256]{2,1,0:T(8,128)(2,1)} async-done(((bf16[32,512,256]{2,1,0:T(8,128)(2,1)}), bf16[32,512,256]{2,1,0:T(8,128)(2,1)}, u32[]{:S(2)}, u32[]{:S(2)}) %all-to-all-start) | async-done | bytes 8388640 | tf_op jit(solution)/shard_map/all_to_all | solution.py:65
  224.7 6.2 %gather_fusion.2 = bf16[16,512,256]{2,1,0:T(8,128)(2,1)} fusion(bf16[32,512,256]{2,1,0:T(8,128)(2,1)} %all-to-all-done, s32[1024]{0:T(1024)S(1)} %pad_clamp_fusion.1), kind=kCustom, calls=%fused_computation.2 | custom fusion | bytes 8388672 | tf_op jit(solution)/shard_map/jit(_take)/gather | solution.py:66
  230.8 6.4 %copy.12 = bf16[16,512,256]{1,2,0:T(8,128)(2,1)} copy(bf16[16,512,256]{2,1,0:T(8,128)(2,1)} %gather_fusion.2) | data formatting | bytes 8388608 | tf_op jit(solution)/shard_map/jit(_take)/gather | solution.py:66
  237.3 6.2 %copy.13 = bf16[16,512,1,2,128]{4,1,0,3,2:T(8,128)(2,1)} copy(bf16[16,512,1,2,128]{1,4,3,0,2:T(8,128)(2,1)} %bitcast.149) | data formatting | bytes 8388608 | tf_op jit(solution)/shard_map/jit(_take)/gather | solution.py:66
  243.5 2.6 broadcast_select_fusion
  246.1 1.2 bitcast_reduce_fusion
  247.4 1.7 fusion.1
  249.1 0.6 fusion.17
  249.7 0.0 slice-start
  249.7 0.5 convolution_bitcast_fusion
  250.3 1.7 fusion.13
  251.9 1.4 slice-done.1
  253.3 8.3 %convolution_convert_fusion = bf16[640,8192]{1,0:T(8,128)(2,1)} fusion(bf16[512,8192]{1,0:T(8,128)(2,1)S(1)} %bitcast.153, bf16[640,512]{1,0:T(8,128)(2,1)S(1)} %bitcast.154, pred[640]{0:T(1024)(128)(4,1)S(1)} %lt.81), kind=kOutput, calls=%fused_computation.6 | convolution fusion | flops 5374279680 | bytes 19530368 | tf_op jit(solution)/shard_map/dot_general | solution.py:74
  261.6 0.0 reduce-scatter.2.cloned.1.call-update
  261.6 0.0 copy-start.1
  261.6 70.3 %reduce-scatter.2.cloned.1.call-done = bf16[80,8192]{1,0:T(8,128)(2,1)} async-done(((bf16[640,8192]{1,0:T(8,128)(2,1)}), bf16[80,8192]{1,0:T(8,128)(2,1)}) %reduce-scatter.2.cloned.1.call-update) | async-done | bytes 1310736 | tf_op jit(solution)/shard_map/reduce_scatter | solution.py:75
  331.9 2.7 add_convert_fusion
  (26 shorter events, 0.2 us)
Async XLA Ops:
  6.5 32.9 %copy-start = (bf16[640,512]{1,0:T(8,128)(2,1)S(1)}, bf16[640,512]{1,0:T(8,128)(2,1)}, u32[]{:S(2)}) copy-start(bf16[640,512]{1,0:T(8,128)(2,1)} %param.8) | copy-start | bytes 1966084
  23.1 11.9 %copy-start.2 = (s32[512]{0:T(512)S(1)}, s32[512]{0:T(512)}, u32[]{:S(2)}) copy-start(s32[512]{0:T(512)} %param.13) | copy-start | bytes 6148
  23.1 15.2 %copy-start.6 = (s32[16,5]{0,1:T(8,128)S(1)}, s32[16,5]{0,1:T(8,128)}, u32[]{:S(2)}) copy-start(s32[16,5]{0,1:T(8,128)} %param.12) | copy-start | bytes 964
  23.1 15.5 %copy-start.3 = (s32[512]{0:T(512)S(1)}, s32[512]{0:T(512)}, u32[]{:S(2)}) copy-start(s32[512]{0:T(512)} %param.11) | copy-start | bytes 6148
  23.1 16.3 %copy-start.5 = (bf16[640,256]{1,0:T(8,128)(2,1)S(1)}, bf16[640,256]{1,0:T(8,128)(2,1)}, u32[]{:S(2)}) copy-start(bf16[640,256]{1,0:T(8,128)(2,1)} %param.9) | copy-start | bytes 983044
  23.1 201.5 %all-to-all-start = ((bf16[32,512,256]{2,1,0:T(8,128)(2,1)}), bf16[32,512,256]{2,1,0:T(8,128)(2,1)}, u32[]{:S(2)}, u32[]{:S(2)}) async-start(bf16[32,512,256]{2,1,0:T(8,128)(2,1)} %scatter_fusion), calls=%async_computation | async-start | bytes 16777216 | tf_op jit(solution)/shard_map/all_to_all | solution.py:65
  34.9 297.0 %reduce-scatter.2.cloned.1.call-start = ((), (), s32[]{:S(2)}) async-start(), calls=%async_computation.2 | async-start | bytes 11796480 | tf_op jit(solution)/shard_map/reduce_scatter | solution.py:75
  249.7 2.2 slice-start
  250.2 3.1 slice-start.1
  261.6 70.3 %copy-start.4 = (bf16[80,8192]{1,0:T(8,128)(2,1)S(1)}, bf16[80,8192]{1,0:T(8,128)(2,1)}, u32[]{:S(2)}) copy-start(bf16[80,8192]{1,0:T(8,128)(2,1)} %param.15) | copy-start | bytes 3932164
  261.6 73.0 %copy-start.1 = (bf16[640,512]{1,0:T(8,128)(2,1)S(1)}, bf16[640,512]{1,0:T(8,128)(2,1)}, u32[]{:S(2)}) copy-start(bf16[640,512]{1,0:T(8,128)(2,1)} %param.8) | copy-start | bytes 1966084
Sparse Core Ops, SparseCore 0:
  261.7 70.1 reduce-scatter.1
where the time goes:
time: 342 us; the launch traced here: 341 us
  waiting for transfers between devices  253 us (74%)
  local copies, waits for them, and re-layouts  40.9 us (12%)
  matrix products  14.7 us (4%)
  between operations  13.6 us (4%)
  starting transfers between devices  11.8 us (3%)
  other arithmetic  7.88 us (2%)
    all_to_all x1, waiting for transfers between devices, per_device(): lax.all_to_all(outgoing, 'dp', split_axis=0, concat_axis=0, tiled=True)  182 us
    reduce_scatter x1, waiting for transfers between devices, per_device(): lax.psum_scatter(partial_sum.astype(jnp.bfloat16), 'tensor', scatter_dime...  70.3 us
    gather x3, local copies, waits for them, and re-layouts, per_device(): jnp.take(incoming, prompt_home, axis=0)  18.8 us
    all_to_all x1, starting transfers between devices, per_device(): lax.all_to_all(outgoing, 'dp', split_axis=0, concat_axis=0, tiled=True)  11.8 us
    scatter x1, local copies, waits for them, and re-layouts, per_device(): jnp.zeros((ndevices, plen_size, kvwidth), jnp.bfloat16).at[score_home]  11 us
    dot_general x1, matrix products, per_device(): partial_sum = jnp.dot(attended, wo, preferred_element_type=jnp.float32)  8.27 us
  transfers between devices with their start and end apart: 2, of which 2 were waited for; matrix products, arithmetic and copies ran while one was open for 2% of the time, Pallas kernels for 0%

commit v1 on v0

v1 whole, which is shorter than its diff:
```python
import functools

import jax
import jax.numpy as jnp
from jax import lax
from jax.experimental import pallas as pl
from jax.experimental.pallas import tpu as pltpu
from jax.sharding import PartitionSpec as P

HD = 128
RESP = 5
TL = 8
GROUPS = ((0, 1), (1, 1), (2, 1), (3, 1), (4, 1))
TN = 512
MESH = pl.DeviceIdType.MESH
LOG2E = 1.4426950408889634
NEG = -1e30


class Dims:
    def __init__(self, ndp, ntensor, pdev, plen, heads, width):
        self.ndp = ndp
        self.ntensor = ntensor
        self.ny = ntensor // 2
        self.pdev = pdev
        self.plen = plen
        self.heads = heads
        self.width = width
        self.tiles = width // TN
        self.half = self.tiles // 2
        self.rows = RESP * heads * TL
        self.qwidth = heads * HD


def bulk_wait(ref, sem):
    pltpu.make_async_copy(ref, ref, sem).wait()


def kernel(dims, refs_layout, *refs):
    names = dict(zip(refs_layout, refs, strict=True))
    idx, rlen, q_ref, own_ref = (names[k] for k in ("idx", "rlen", "q", "own"))
    kv_hbm, wo_hbm, res_hbm, out_ref = (names[k] for k in ("kv_hbm", "wo_hbm", "res_hbm", "out"))
    qv, kv, wo, res, fin = (names[k] for k in ("qv", "kv", "wo", "res", "fin"))
    orr, lser, ob, st_t, att = (names[k] for k in ("orr", "lser", "ob", "st_t", "att"))
    load_sem, z_sem, core_sem, ring_sem = (names[k] for k in ("load_sem", "z_sem", "core_sem", "ring_sem"))
    ndp, ny, pdev, heads = dims.ndp, dims.ny, dims.pdev, dims.heads
    tiles, half = dims.tiles, dims.half
    seg = heads * TL
    f32, bf16 = jnp.float32, jnp.bfloat16
    me = lax.axis_index("dp")
    tensor = lax.axis_index("tensor")
    ypos, core = tensor // 2, lax.rem(tensor, 2)
    partner = ypos * 2 + 1 - core
    y_next = lax.rem(ypos + 1, ny) * 2 + core
    y_prev = lax.rem(ypos + ny - 1, ny) * 2 + core
    o_from, o_home, o_qidx, o_back = 0, pdev, 2 * pdev, 2 * pdev + ndp
    o_plen = 2 * pdev + 2 * ndp
    cc = HD ** (-0.5) * LOG2E

    loads = [pltpu.make_async_copy(kv_hbm, kv, load_sem.at[0]), pltpu.make_async_copy(res_hbm, res, load_sem.at[1])]
    loads += [
        pltpu.make_async_copy(wo_hbm.at[:, pl.ds(n * TN, TN)], wo.at[n], load_sem.at[2 + n]) for n in range(tiles)
    ]
    for load in loads:
        load.start()

    barrier = pltpu.get_barrier_semaphore()

    def greet(k, carry):
        pl.semaphore_signal(barrier, inc=1, device_id=(lax.rem(me + k, ndp), tensor), device_id_type=MESH)
        return carry

    lax.fori_loop(1, ndp, greet, 0)
    for other in (partner, y_next, y_prev):
        pl.semaphore_signal(barrier, inc=1, device_id=(me, other), device_id_type=MESH)

    def turn(i, carry):
        x = q_ref[pl.ds(pl.multiple_of(i * 2 * RESP * TL, 2 * RESP * TL), 2 * RESP * TL), :].astype(f32)
        for part in range(2):
            pieces = [
                x[(part * RESP + r) * TL : (part * RESP + r + 1) * TL, h * HD : (h + 1) * HD]
                for r in range(RESP)
                for h in range(heads)
            ]
            qv[i * 2 + part] = jnp.concatenate(pieces, axis=0).astype(bf16)
        return carry

    lax.fori_loop(0, pdev // 2, turn, 0)
    pl.semaphore_wait(barrier, ndp - 1 + 3)

    def q_send(g):
        r0, size = GROUPS[g]
        qs, qr = names["qs", g], names["qr", g]
        span = pl.ds(r0 * seg, size * seg)

        def fill(h, carry):
            qs[h] = qv[idx[o_qidx + h], span, :]
            return carry

        lax.fori_loop(0, ndp, fill, 0)

        def send(k, carry):
            target = lax.rem(me + k, ndp)
            pltpu.make_async_remote_copy(
                src_ref=qs.at[target], dst_ref=qr.at[me], send_sem=z_sem.at[g, 0], recv_sem=z_sem.at[g, 1],
                device_id=(target, tensor), device_id_type=MESH,
            ).start()
            return carry

        lax.fori_loop(1, ndp, send, 0)
        qr[me] = qs[me]

    def own_part():
        n = 2 * dims.rows
        cols = 2 * RESP * TL
        row = lax.broadcasted_iota(jnp.int32, (n, cols), 0)
        col = lax.broadcasted_iota(jnp.int32, (n, cols), 1)
        seg_bits = (seg - 1).bit_length()
        seen = ((row >> seg_bits) == (col >> 3)) & ((col & 7) <= (row & 7))
        lane = lax.broadcasted_iota(jnp.int32, (dims.rows, 128), 1)

        def one(i, stat):
            x = own_ref[pl.ds(pl.multiple_of(i * cols, cols), cols), :]
            qp = jnp.concatenate([qv[i * 2], qv[i * 2 + 1]], axis=0)
            s = lax.dot_general(qp, x[:, :HD], (((1,), (1,)), ((), ())), preferred_element_type=f32)
            s = jnp.where(seen, s * cc, NEG)
            m = jnp.max(s, axis=1, keepdims=True)
            p = jnp.exp2(s - m)
            l = jnp.sum(p, axis=1, keepdims=True)
            o = jnp.dot(p.astype(bf16), x[:, HD:], preferred_element_type=f32) / l
            lse = m + jnp.log2(l)
            for part in range(2):
                cut = slice(part * dims.rows, (part + 1) * dims.rows)
                orr[i * 2 + part] = o[cut]
                stat = jnp.where(lane == i * 2 + part, lse[cut], stat)
            return stat

        lser[...] = lax.fori_loop(0, pdev // 2, one, jnp.zeros((dims.rows, 128), f32))

    def attend(g):
        size = GROUPS[g][1]
        n = size * seg
        qr = names["qr", g]
        bulk_wait(qr.at[pl.ds(0, ndp - 1)], z_sem.at[g, 1])
        col = lax.broadcasted_iota(jnp.int32, (n, dims.plen), 1)
        lane = lax.broadcasted_iota(jnp.int32, (n, 128), 1)

        def one(j, stat):
            qj = qr[idx[o_from + j]]
            s = lax.dot_general(qj, kv[j, :, :HD], (((1,), (1,)), ((), ())), preferred_element_type=f32)
            s = jnp.where(col < idx[o_plen + j], s * cc, NEG)
            m = jnp.max(s, axis=1, keepdims=True)
            p = jnp.exp2(s - m)
            l = jnp.sum(p, axis=1, keepdims=True)
            o = jnp.dot(p.astype(bf16), kv[j, :, HD:], preferred_element_type=f32) / l
            ob[j, pl.ds(0, n), :] = o.astype(bf16)
            return jnp.where(lane == j, m + jnp.log2(l), stat)

        stat = lax.fori_loop(0, pdev, one, jnp.zeros((n, 128), f32))
        for b in range(-(-n // 128)):
            block = stat[b * 128 : (b + 1) * 128]
            if block.shape[0] < 128:
                block = jnp.concatenate([block, jnp.zeros((128 - block.shape[0], 128), f32)], axis=0)
            st_t[:, pl.ds(b * 128, 128)] = jnp.transpose(block)[:pdev]

    def a_send(g):
        n = GROUPS[g][1] * seg
        as_, ar, ss, sr = (names[k, g] for k in ("as", "ar", "ss", "sr"))
        lanes = ss.shape[2]

        def fill(s, carry):
            j = idx[o_back + s]
            as_[s] = ob[j, pl.ds(0, n), :]
            ss[s] = st_t[pl.ds(j, 1), pl.ds(0, lanes)]
            return carry

        lax.fori_loop(0, ndp, fill, 0)

        def send(k, carry):
            target = lax.rem(me + k, ndp)
            for src, dst, at in ((as_, ar, 2), (ss, sr, 4)):
                pltpu.make_async_remote_copy(
                    src_ref=src.at[target], dst_ref=dst.at[me], send_sem=z_sem.at[g, at],
                    recv_sem=z_sem.at[g, at + 1], device_id=(target, tensor), device_id_type=MESH,
                ).start()
            return carry

        lax.fori_loop(1, ndp, send, 0)
        ar[me] = as_[me]
        sr[me] = ss[me]

    def merge(g):
        r0, size = GROUPS[g]
        n = size * seg
        ar, sr = names["ar", g], names["sr", g]
        bulk_wait(ar.at[pl.ds(0, ndp - 1)], z_sem.at[g, 3])
        bulk_wait(sr.at[pl.ds(0, ndp - 1)], z_sem.at[g, 5])
        homes = [idx[o_home + i] for i in range(pdev)]
        stat = jnp.concatenate([sr[homes[i]] for i in range(pdev)], axis=0)
        blocks = []
        for b in range(-(-n // 128)):
            block = jnp.concatenate([stat[:, b * 128 : (b + 1) * 128], jnp.zeros((128 - pdev, 128), f32)], axis=0)
            blocks.append(jnp.transpose(block))
        lp = jnp.concatenate(blocks, axis=0)[:n] if len(blocks) > 1 else blocks[0][:n]
        lr = lser[pl.ds(r0 * seg, n), :]
        w = 1.0 / (1.0 + jnp.exp2(lr - lp))
        position = lax.broadcasted_iota(jnp.int32, (seg, HD), 0) & 7
        for i in range(0, pdev, 2):
            pieces = [[], []]
            for part in range(2):
                wi = w[:, i + part : i + part + 1]
                op = ar[homes[i + part]].astype(f32)
                both = wi * op + (1.0 - wi) * orr[i + part, pl.ds(r0 * seg, n), :]
                for r in range(size):
                    x = both[r * seg : (r + 1) * seg]
                    x = jnp.where(position < rlen[i + part, r0 + r], x, 0.0)
                    x = jnp.concatenate([x[h * TL : (h + 1) * TL] for h in range(heads)], axis=1)
                    pieces[part].append(x)
            rows = [pieces[part][r] for r in range(size) for part in range(2)]
            owner = i // 2
            att[lax.rem(owner + core, 2), owner // 2, pl.ds(0, 2 * TL * size), :] = jnp.concatenate(rows, axis=0).astype(bf16)

    def project(g):
        size = GROUPS[g][1]
        n = 2 * TL * size
        cs, cr, po = (names[k, g] for k in ("cs", "cr", "po"))
        a = att[:, :, pl.ds(0, n), :].reshape(2 * ny * n, dims.qwidth)

        def tile(i, carry):
            x = jnp.dot(a, wo[i], preferred_element_type=f32).astype(bf16)
            cs[i] = x[ny * n :].reshape(ny, n, TN)
            pltpu.make_async_remote_copy(
                src_ref=cs.at[i], dst_ref=cr.at[i], send_sem=core_sem.at[g, 0], recv_sem=core_sem.at[g, 1],
                device_id=(me, partner), device_id_type=MESH,
            ).start()
            po[i] = x[: ny * n].reshape(ny, n, TN)
            return carry

        lax.fori_loop(0, tiles, tile, 0)

    def ring_copy(g, step, way):
        rs, rr = names["rs", g], names["rr", g]
        return pltpu.make_async_remote_copy(
            src_ref=rs.at[way, step], dst_ref=rr.at[way, step], send_sem=ring_sem.at[g, way, step, 0],
            recv_sem=ring_sem.at[g, way, step, 1], device_id=(me, y_next if way == 0 else y_prev), device_id_type=MESH,
        )

    def ring(g, step):
        cr, po, rs, rr = (names[k, g] for k in ("cr", "po", "rs", "rr"))
        if step == 0:
            bulk_wait(cr, core_sem.at[g, 1])
        for way in range(2):
            if step > 0:
                ring_copy(g, step - 1, way).wait_recv()
            chunk = lax.rem(ypos + ny - 1 - step, ny) if way == 0 else lax.rem(ypos + 1 + step, ny)

            def tile(i, carry):
                n = way * half + i
                x = po[n, chunk].astype(f32) + cr[n, chunk].astype(f32)
                if step > 0:
                    x = x + rr[way, step - 1, i].astype(f32)
                rs[way, step, i] = x.astype(bf16)
                return carry

            lax.fori_loop(0, half, tile, 0)
            ring_copy(g, step, way).start()

    def finish(g):
        r0, size = GROUPS[g]
        cr, po, rr = (names[k, g] for k in ("cr", "po", "rr"))
        for way in range(2):
            ring_copy(g, ny - 2, way).wait_recv()

            def tile(i, carry):
                n = way * half + i
                x = po[n, ypos].astype(f32) + cr[n, ypos].astype(f32) + rr[way, ny - 2, i].astype(f32)
                at = pl.ds(pl.multiple_of(n * TN, TN), TN)
                for r in range(size):
                    for part in range(2):
                        down = pl.ds(part * RESP * TL + (r0 + r) * TL, TL)
                        fin[down, at] = fin[down, at] + x[(r * 2 + part) * TL : (r * 2 + part + 1) * TL]
                return carry

            lax.fori_loop(0, half, tile, 0)

    def columns(body):
        def tile(n, carry):
            body(pl.ds(pl.multiple_of(n * TN, TN), TN))
            return carry

        lax.fori_loop(0, tiles, tile, 0)

    def start_total(at):
        fin[:, at] = res[:, at].astype(f32)

    def end_total(at):
        out_ref[:, at] = fin[:, at].astype(bf16)

    ng = len(GROUPS)
    q_send(0)
    if ng > 1:
        q_send(1)
    own_part()
    loads[1].wait()
    columns(start_total)
    loads[0].wait()
    for slot in range(ng + 3):
        if slot < ng:
            attend(slot)
            a_send(slot)
            if slot + 2 < ng:
                q_send(slot + 2)
        if 0 <= slot - 3 < ng:
            finish(slot - 3)
        if 0 <= slot - 2 < ng:
            ring(slot - 2, 1)
        if 0 <= slot - 1 < ng:
            merge(slot - 1)
            if slot == 1:
                for load in loads[2:]:
                    load.wait()
            project(slot - 1)
        if 0 <= slot - 2 < ng:
            ring(slot - 2, 2)
        if 0 <= slot - 1 < ng:
            ring(slot - 1, 0)
    columns(end_total)

    for g in range(ng):
        bulk_wait(names["qs", g].at[pl.ds(0, ndp - 1)], z_sem.at[g, 0])
        bulk_wait(names["as", g].at[pl.ds(0, ndp - 1)], z_sem.at[g, 2])
        bulk_wait(names["ss", g].at[pl.ds(0, ndp - 1)], z_sem.at[g, 4])
        bulk_wait(names["cs", g], core_sem.at[g, 0])
        for step in range(ny - 1):
            for way in range(2):
                ring_copy(g, step, way).wait_send()


def per_device(queries, resp_kv, prompt_kv, prompt_len, resp_len, dest, wo, residual):
    ndp, ntensor = lax.axis_size("dp"), lax.axis_size("tensor")
    me = lax.axis_index("dp")
    pdev, plen, _ = prompt_kv.shape
    heads = queries.shape[1] // HD
    width = wo.shape[1]
    total = dest.shape[0]
    dims = Dims(ndp, ntensor, pdev, plen, heads, width)
    ny, tiles, half = dims.ny, dims.tiles, dims.half
    seg = heads * TL

    slots = me * pdev + jnp.arange(pdev, dtype=jnp.int32)
    every = jnp.arange(total, dtype=jnp.int32)
    home = jnp.sum(jnp.where(dest[None, :] == slots[:, None], every[None, :], 0), axis=1) // pdev
    scorer = lax.dynamic_slice(dest, (me * pdev,), (pdev,)) // pdev
    live = lax.dynamic_slice(prompt_len, (me * pdev,), (pdev,))
    here = jnp.arange(pdev, dtype=jnp.int32)
    devices = jnp.arange(ndp, dtype=jnp.int32)
    qidx = jnp.sum(jnp.where(home[None, :] == devices[:, None], here[None, :], 0), axis=1)
    back = jnp.sum(jnp.where(scorer[None, :] == devices[:, None], here[None, :], 0), axis=1)
    idx = jnp.concatenate([scorer, home, qidx, back, live]).astype(jnp.int32)

    bf16, f32 = jnp.bfloat16, jnp.float32
    layout = ["idx", "rlen", "q", "own", "kv_hbm", "wo_hbm", "res_hbm", "out"]
    scratch = []

    def add(name, shape):
        layout.append(name)
        scratch.append(shape)

    add("qv", pltpu.VMEM((pdev, dims.rows, HD), bf16))
    add("kv", pltpu.VMEM(prompt_kv.shape, bf16))
    add("wo", pltpu.VMEM((tiles, wo.shape[0], TN), bf16))
    add("res", pltpu.VMEM(residual.shape, bf16))
    add("fin", pltpu.VMEM(residual.shape, f32))
    add("orr", pltpu.VMEM((pdev, dims.rows, HD), f32))
    add("lser", pltpu.VMEM((dims.rows, 128), f32))
    most = max(size for _, size in GROUPS)
    add("ob", pltpu.VMEM((pdev, most * seg, HD), bf16))
    add("st_t", pltpu.VMEM((pdev, -(-most * seg // 128) * 128), f32))
    add("att", pltpu.VMEM((2, ny, most * 2 * TL, dims.qwidth), bf16))
    for g, (_, size) in enumerate(GROUPS):
        n = size * seg
        for name in ("qs", "qr", "as", "ar"):
            add((name, g), pltpu.VMEM((ndp, n, HD), bf16))
        for name in ("ss", "sr"):
            add((name, g), pltpu.VMEM((ndp, 1, -(-n // 128) * 128), f32))
        for name in ("cs", "cr", "po"):
            add((name, g), pltpu.VMEM((tiles, ny, 2 * TL * size, TN), bf16))
        for name in ("rs", "rr"):
            add((name, g), pltpu.VMEM((2, ny - 1, half, 2 * TL * size, TN), bf16))
    ng = len(GROUPS)
    add("load_sem", pltpu.SemaphoreType.DMA((2 + tiles,)))
    add("z_sem", pltpu.SemaphoreType.DMA((ng, 6)))
    add("core_sem", pltpu.SemaphoreType.DMA((ng, 2)))
    add("ring_sem", pltpu.SemaphoreType.DMA((ng, 2, ny - 1, 2)))

    smem = pl.BlockSpec(memory_space=pltpu.SMEM)
    vmem = pl.BlockSpec(memory_space=pltpu.VMEM)
    hbm = pl.BlockSpec(memory_space=pl.ANY)
    return pl.pallas_call(
        functools.partial(kernel, dims, layout),
        out_shape=jax.ShapeDtypeStruct(residual.shape, bf16),
        in_specs=[smem, smem, vmem, vmem, hbm, hbm, hbm],
        out_specs=vmem,
        scratch_shapes=scratch,
        compiler_params=pltpu.CompilerParams(
            collective_id=0, has_side_effects=True, vmem_limit_bytes=60 * 2**20
        ),
    )(idx, resp_len, queries, resp_kv, prompt_kv, wo, residual)


def solution(mesh):
    in_specs = (
        P("dp", "tensor"),
        P("dp", "tensor"),
        P("dp", None, "tensor"),
        P(),
        P("dp", None),
        P(),
        P("tensor", None),
        P(("dp", "tensor"), None),
    )
    out_specs = P(("dp", "tensor"), None)
    return jax.shard_map(
        per_device, mesh=mesh, in_specs=in_specs, out_specs=out_specs, check_vma=False
    )
```

time: 342 us -> 123 us (0.36)
  waiting for transfers between devices: 253 us -> 0 us
  Pallas kernels: 0 us -> 116 us
  local copies, waits for them, and re-layouts: 40.9 us -> 5.2 us
  matrix products: 14.7 us -> 0 us
  between operations: 13.6 us -> 0.01 us
  starting transfers between devices: 11.8 us -> 0 us
  other arithmetic: 7.88 us -> 1.73 us
    all_to_all x1 -> x0, waiting for transfers between devices: 182 us -> none  [per_device(): lax.all_to_all(outgoing, 'dp', split_axis=0, concat_axis=0, tiled=True)]
    pallas_call x0 -> x1, Pallas kernels: none -> 116 us  [per_device(): pl.pallas_call(functools.partial(kernel, dims, layout), out_shape=jax.Sha...]
    reduce_scatter x1 -> x0, waiting for transfers between devices: 70.3 us -> none  [per_device(): lax.psum_scatter(partial_sum.astype(jnp.bfloat16), 'tensor', scatter_dime...]
    gather x6 -> x0, local copies, waits for them, and re-layouts: 21.5 us -> none  [the longest x3 18.8 us: per_device(): jnp.take(incoming, prompt_home, axis=0)]
    dot_general x5 -> x0, matrix products: 14.7 us -> none  [the longest x1 8.27 us: per_device(): partial_sum = jnp.dot(attended, wo, preferred_element_type=jnp.float32)]
    scatter x2 -> x0, local copies, waits for them, and re-layouts: 13.6 us -> none  [the longest x1 11 us: per_device(): jnp.zeros((ndevices, plen_size, kvwidth), jnp.bfloat16).at[score_home]]
    all_to_all x1 -> x0, starting transfers between devices: 11.8 us -> none  [per_device(): lax.all_to_all(outgoing, 'dp', split_axis=0, concat_axis=0, tiled=True)]
    broadcast_in_dim x1 -> x0, local copies, waits for them, and re-layouts: 4.16 us -> none  [per_device(): jnp.zeros((ndevices, plen_size, kvwidth), jnp.bfloat16).at[score_home]]
  transfers between devices with their start and end apart: 2 -> 0, of which waited for: 2 -> 0; matrix products, arithmetic and copies ran while one was open for 2% -> 0% of each run, Pallas kernels for 0% -> 0%
where the time goes in v1:
time: 123 us
  Pallas kernels  116 us (94%)
  local copies, waits for them, and re-layouts  5.2 us (4%)
  other arithmetic  1.73 us (1%)
    pallas_call x1, Pallas kernels, per_device(): pl.pallas_call(functools.partial(kernel, dims, layout), out_shape=jax.Sha...  116 us
    unnamed x2, local copies, waits for them, and re-layouts  3.82 us

profile of v1, /device:TPU:2, one launch (start us, length us, event | category | flops | bytes accessed | tf_op | source)
XLA Modules:
  0.0 122.8 jit_solution(10581658865231329049)
XLA Ops:
  0.0 0.9 select_reduce_fusion
  0.9 0.8 and_select_fusion.1
  1.6 0.8 dynamic_slice.7
  2.4 0.1 select_reduce_fusion.1
  2.5 0.6 concatenate.3.refs_0_
  3.1 1.4 %copy.10.refs_1_ = s32[16,5]{1,0:T(8,128)} copy(s32[16,5]{0,1:T(8,128)} %param.12) | data formatting | bytes 640 | tf_op args[4]
  4.5 115.9 %shard_map.82 = bf16[80,8192]{1,0:T(8,128)(2,1)} custom-call(s32[112]{0:T(128)} %concatenate.3.refs_0_, s32[16,5]{1,0:T(8,128)} %copy.10.refs_1_, bf16[640,512]{1,0:T(8,128)(2,1)} %refs_2_.1, bf16[640,256]{1,0:T(8,128)(2,1)} %refs_3_.1, bf16[16,512,256]{2,1,0:T(8,128)(2,1)} %refs_4_.1, bf16[512,8192]{1,0:T(8,128)(2,1)} %refs_5_.1, bf16[80,8192]{1,0:T(8,128)(2,1)} %refs_6_.1), custom_call_target="tpu_custom_call" | custom-call | tf_op jit(solution)/shard_map/pallas_call | solution.py:399
  120.4 2.5 %copy.12 = bf16[80,8192]{1,0:T(8,128)(2,1)} copy(bf16[80,8192]{1,0:T(8,128)(2,1)} %shard_map.82) | data formatting | bytes 2621440
  (2 shorter events, 0.0 us)

commit v2 on v1

--- a/solution.py
+++ b/solution.py
@@ -12,6 +12,9 @@
 TL = 8
 GROUPS = ((0, 1), (1, 1), (2, 1), (3, 1), (4, 1))
 TN = 512
+SCOPES = False
+ATT_UNROLL = 4
+PROJ_UNROLL = 4
 MESH = pl.DeviceIdType.MESH
 LOG2E = 1.4426950408889634
 NEG = -1e30
@@ -39,8 +42,9 @@
 def kernel(dims, refs_layout, *refs):
     names = dict(zip(refs_layout, refs, strict=True))
     idx, rlen, q_ref, own_ref = (names[k] for k in ("idx", "rlen", "q", "own"))
+    dest, live = names["dest"], names["live"]
     kv_hbm, wo_hbm, res_hbm, out_ref = (names[k] for k in ("kv_hbm", "wo_hbm", "res_hbm", "out"))
-    qv, kv, wo, res, fin = (names[k] for k in ("qv", "kv", "wo", "res", "fin"))
+    qv, kv, kt, wo, res, fin = (names[k] for k in ("qv", "kv", "kt", "wo", "res", "fin"))
     orr, lser, ob, st_t, att = (names[k] for k in ("orr", "lser", "ob", "st_t", "att"))
     load_sem, z_sem, core_sem, ring_sem = (names[k] for k in ("load_sem", "z_sem", "core_sem", "ring_sem"))
     ndp, ny, pdev, heads = dims.ndp, dims.ny, dims.pdev, dims.heads
@@ -53,8 +57,7 @@
     partner = ypos * 2 + 1 - core
     y_next = lax.rem(ypos + 1, ny) * 2 + core
     y_prev = lax.rem(ypos + ny - 1, ny) * 2 + core
-    o_from, o_home, o_qidx, o_back = 0, pdev, 2 * pdev, 2 * pdev + ndp
-    o_plen = 2 * pdev + 2 * ndp
+    o_home, o_qidx, o_back = 0, pdev, pdev + ndp
     cc = HD ** (-0.5) * LOG2E
 
     loads = [pltpu.make_async_copy(kv_hbm, kv, load_sem.at[0]), pltpu.make_async_copy(res_hbm, res, load_sem.at[1])]
@@ -86,7 +89,9 @@
         return carry
 
     lax.fori_loop(0, pdev // 2, turn, 0)
-    pl.semaphore_wait(barrier, ndp - 1 + 3)
+
+    def all_here():
+        pl.semaphore_wait(barrier, ndp - 1 + 3)
 
     def q_send(g):
         r0, size = GROUPS[g]
@@ -109,6 +114,15 @@
 
         lax.fori_loop(1, ndp, send, 0)
         qr[me] = qs[me]
+
+    def turn_keys():
+        loads[0].wait()
+
+        def one(j, carry):
+            kt[j] = jnp.transpose(kv[j, :, :HD])
+            return carry
+
+        lax.fori_loop(0, pdev, one, 0, unroll=2)
 
     def own_part():
         n = 2 * dims.rows
@@ -137,18 +151,20 @@
 
         lser[...] = lax.fori_loop(0, pdev // 2, one, jnp.zeros((dims.rows, 128), f32))
 
+    def q_wait(g):
+        bulk_wait(names["qr", g].at[pl.ds(0, ndp - 1)], z_sem.at[g, 1])
+
     def attend(g):
         size = GROUPS[g][1]
         n = size * seg
         qr = names["qr", g]
-        bulk_wait(qr.at[pl.ds(0, ndp - 1)], z_sem.at[g, 1])
         col = lax.broadcasted_iota(jnp.int32, (n, dims.plen), 1)
         lane = lax.broadcasted_iota(jnp.int32, (n, 128), 1)
 
         def one(j, stat):
-            qj = qr[idx[o_from + j]]
-            s = lax.dot_general(qj, kv[j, :, :HD], (((1,), (1,)), ((), ())), preferred_element_type=f32)
-            s = jnp.where(col < idx[o_plen + j], s * cc, NEG)
+            qj = qr[dest[me * pdev + j] // pdev]
+            s = jnp.dot(qj, kt[j], preferred_element_type=f32)
+            s = jnp.where(col < live[me * pdev + j], s * cc, NEG)
             m = jnp.max(s, axis=1, keepdims=True)
             p = jnp.exp2(s - m)
             l = jnp.sum(p, axis=1, keepdims=True)
@@ -156,7 +172,7 @@
             ob[j, pl.ds(0, n), :] = o.astype(bf16)
             return jnp.where(lane == j, m + jnp.log2(l), stat)
 
-        stat = lax.fori_loop(0, pdev, one, jnp.zeros((n, 128), f32))
+        stat = lax.fori_loop(0, pdev, one, jnp.zeros((n, 128), f32), unroll=ATT_UNROLL)
         for b in range(-(-n // 128)):
             block = stat[b * 128 : (b + 1) * 128]
             if block.shape[0] < 128:
@@ -189,12 +205,14 @@
         ar[me] = as_[me]
         sr[me] = ss[me]
 
+    def a_wait(g):
+        bulk_wait(names["ar", g].at[pl.ds(0, ndp - 1)], z_sem.at[g, 3])
+        bulk_wait(names["sr", g].at[pl.ds(0, ndp - 1)], z_sem.at[g, 5])
+
     def merge(g):
         r0, size = GROUPS[g]
         n = size * seg
         ar, sr = names["ar", g], names["sr", g]
-        bulk_wait(ar.at[pl.ds(0, ndp - 1)], z_sem.at[g, 3])
-        bulk_wait(sr.at[pl.ds(0, ndp - 1)], z_sem.at[g, 5])
         homes = [idx[o_home + i] for i in range(pdev)]
         stat = jnp.concatenate([sr[homes[i]] for i in range(pdev)], axis=0)
         blocks = []
@@ -213,14 +231,14 @@
                 both = wi * op + (1.0 - wi) * orr[i + part, pl.ds(r0 * seg, n), :]
                 for r in range(size):
                     x = both[r * seg : (r + 1) * seg]
-                    x = jnp.where(position < rlen[i + part, r0 + r], x, 0.0)
+                    x = jnp.where(position < rlen[r0 + r, i + part], x, 0.0)
                     x = jnp.concatenate([x[h * TL : (h + 1) * TL] for h in range(heads)], axis=1)
                     pieces[part].append(x)
             rows = [pieces[part][r] for r in range(size) for part in range(2)]
             owner = i // 2
             att[lax.rem(owner + core, 2), owner // 2, pl.ds(0, 2 * TL * size), :] = jnp.concatenate(rows, axis=0).astype(bf16)
 
-    def project(g):
+    def project(g, way):
         size = GROUPS[g][1]
         n = 2 * TL * size
         cs, cr, po = (names[k, g] for k in ("cs", "cr", "po"))
@@ -230,58 +248,73 @@
             x = jnp.dot(a, wo[i], preferred_element_type=f32).astype(bf16)
             cs[i] = x[ny * n :].reshape(ny, n, TN)
             pltpu.make_async_remote_copy(
-                src_ref=cs.at[i], dst_ref=cr.at[i], send_sem=core_sem.at[g, 0], recv_sem=core_sem.at[g, 1],
+                src_ref=cs.at[i], dst_ref=cr.at[i], send_sem=core_sem.at[g, way, 0], recv_sem=core_sem.at[g, way, 1],
                 device_id=(me, partner), device_id_type=MESH,
             ).start()
             po[i] = x[: ny * n].reshape(ny, n, TN)
             return carry
 
-        lax.fori_loop(0, tiles, tile, 0)
-
-    def ring_copy(g, step, way):
-        rs, rr = names["rs", g], names["rr", g]
+        lax.fori_loop(way * half, (way + 1) * half, tile, 0, unroll=PROJ_UNROLL)
+
+    def core_wait(g, way):
+        bulk_wait(names["cr", g].at[pl.ds(way * half, half)], core_sem.at[g, way, 1])
+
+    def across(y, way):
+        return y + 1 - 2 * lax.rem(y, 2) if way == 0 else ny - 1 - y
+
+    def y_copy(g, step, way):
+        send, recv = (names[k, g] for k in (("xs", "xr"), ("ws", "wr"))[step])
+        other = across(ypos, way if step == 0 else 1 - way) * 2 + core
         return pltpu.make_async_remote_copy(
-            src_ref=rs.at[way, step], dst_ref=rr.at[way, step], send_sem=ring_sem.at[g, way, step, 0],
-            recv_sem=ring_sem.at[g, way, step, 1], device_id=(me, y_next if way == 0 else y_prev), device_id_type=MESH,
+            src_ref=send.at[way], dst_ref=recv.at[way], send_sem=ring_sem.at[g, way, step, 0],
+            recv_sem=ring_sem.at[g, way, step, 1], device_id=(me, other), device_id_type=MESH,
         )
 
-    def ring(g, step):
-        cr, po, rs, rr = (names[k, g] for k in ("cr", "po", "rs", "rr"))
-        if step == 0:
-            bulk_wait(cr, core_sem.at[g, 1])
-        for way in range(2):
-            if step > 0:
-                ring_copy(g, step - 1, way).wait_recv()
-            chunk = lax.rem(ypos + ny - 1 - step, ny) if way == 0 else lax.rem(ypos + 1 + step, ny)
-
-            def tile(i, carry):
-                n = way * half + i
-                x = po[n, chunk].astype(f32) + cr[n, chunk].astype(f32)
-                if step > 0:
-                    x = x + rr[way, step - 1, i].astype(f32)
-                rs[way, step, i] = x.astype(bf16)
-                return carry
-
-            lax.fori_loop(0, half, tile, 0)
-            ring_copy(g, step, way).start()
-
-    def finish(g):
+    def both_cores(g, n, owner):
+        return names["po", g][n, owner].astype(f32) + names["cr", g][n, owner].astype(f32)
+
+    def y_first(g, way):
+        xs = names["xs", g]
+        other = across(ypos, way)
+        owners = (other, across(other, 1 - way))
+
+        def tile(i, carry):
+            for k in range(2):
+                xs[way, k, i] = both_cores(g, way * half + i, owners[k]).astype(bf16)
+            return carry
+
+        lax.fori_loop(0, half, tile, 0, unroll=2)
+        y_copy(g, 0, way).start()
+
+    def y_wait(g, step, way):
+        y_copy(g, step, way).wait_recv()
+
+    def y_second(g, way):
+        xr, ws = names["xr", g], names["ws", g]
+        owner = across(ypos, 1 - way)
+
+        def tile(i, carry):
+            ws[way, i] = (both_cores(g, way * half + i, owner) + xr[way, 1, i].astype(f32)).astype(bf16)
+            return carry
+
+        lax.fori_loop(0, half, tile, 0, unroll=2)
+        y_copy(g, 1, way).start()
+
+    def finish(g, way):
         r0, size = GROUPS[g]
-        cr, po, rr = (names[k, g] for k in ("cr", "po", "rr"))
-        for way in range(2):
-            ring_copy(g, ny - 2, way).wait_recv()
-
-            def tile(i, carry):
-                n = way * half + i
-                x = po[n, ypos].astype(f32) + cr[n, ypos].astype(f32) + rr[way, ny - 2, i].astype(f32)
-                at = pl.ds(pl.multiple_of(n * TN, TN), TN)
-                for r in range(size):
-                    for part in range(2):
-                        down = pl.ds(part * RESP * TL + (r0 + r) * TL, TL)
-                        fin[down, at] = fin[down, at] + x[(r * 2 + part) * TL : (r * 2 + part + 1) * TL]
-                return carry
-
-            lax.fori_loop(0, half, tile, 0)
+        xr, wr = names["xr", g], names["wr", g]
+
+        def tile(i, carry):
+            n = way * half + i
+            x = both_cores(g, n, ypos) + xr[way, 0, i].astype(f32) + wr[way, i].astype(f32)
+            at = pl.ds(pl.multiple_of(n * TN, TN), TN)
+            for r in range(size):
+                for part in range(2):
+                    down = pl.ds(part * RESP * TL + (r0 + r) * TL, TL)
+                    fin[down, at] = fin[down, at] + x[(r * 2 + part) * TL : (r * 2 + part + 1) * TL]
+            return carry
+
+        lax.fori_loop(0, half, tile, 0, unroll=2)
 
     def columns(body):
         def tile(n, carry):
@@ -297,43 +330,68 @@
         out_ref[:, at] = fin[:, at].astype(bf16)
 
     ng = len(GROUPS)
-    q_send(0)
+
+    def loaded():
+        for load in loads[2:]:
+            load.wait()
+
+    def total_of_residual():
+        loads[1].wait()
+        columns(start_total)
+
+    def run(step, *args):
+        if SCOPES:
+            with jax.named_scope("_".join([step.__name__, *map(str, args)])):
+                step(*args)
+        else:
+            step(*args)
+
+    run(all_here)
+    run(q_send, 0)
     if ng > 1:
-        q_send(1)
-    own_part()
-    loads[1].wait()
-    columns(start_total)
-    loads[0].wait()
-    for slot in range(ng + 3):
+        run(q_send, 1)
+    run(turn_keys)
+    run(own_part)
+    run(total_of_residual)
+    for slot in range(ng + 2):
         if slot < ng:
-            attend(slot)
-            a_send(slot)
+            run(q_wait, slot)
+            run(attend, slot)
+            run(a_send, slot)
             if slot + 2 < ng:
-                q_send(slot + 2)
-        if 0 <= slot - 3 < ng:
-            finish(slot - 3)
-        if 0 <= slot - 2 < ng:
-            ring(slot - 2, 1)
+                run(q_send, slot + 2)
+        if 0 <= slot - 3:
+            for way in range(2):
+                run(y_wait, slot - 3, 1, way)
+                run(finish, slot - 3, way)
         if 0 <= slot - 1 < ng:
-            merge(slot - 1)
+            run(a_wait, slot - 1)
+            run(merge, slot - 1)
             if slot == 1:
-                for load in loads[2:]:
-                    load.wait()
-            project(slot - 1)
-        if 0 <= slot - 2 < ng:
-            ring(slot - 2, 2)
+                run(loaded)
+            run(project, slot - 1, 0)
+            run(project, slot - 1, 1)
+        if 0 <= slot - 2:
+            for way in range(2):
+                run(y_wait, slot - 2, 0, way)
+                run(y_second, slot - 2, way)
         if 0 <= slot - 1 < ng:
-            ring(slot - 1, 0)
+            for way in range(2):
+                run(core_wait, slot - 1, way)
+                run(y_first, slot - 1, way)
+    for way in range(2):
+        run(y_wait, ng - 1, 1, way)
+        run(finish, ng - 1, way)
     columns(end_total)
 
     for g in range(ng):
         bulk_wait(names["qs", g].at[pl.ds(0, ndp - 1)], z_sem.at[g, 0])
         bulk_wait(names["as", g].at[pl.ds(0, ndp - 1)], z_sem.at[g, 2])
         bulk_wait(names["ss", g].at[pl.ds(0, ndp - 1)], z_sem.at[g, 4])
-        bulk_wait(names["cs", g], core_sem.at[g, 0])
-        for step in range(ny - 1):
-            for way in range(2):
-                ring_copy(g, step, way).wait_send()
+        for way in range(2):
+            bulk_wait(names["cs", g].at[pl.ds(way * half, half)], core_sem.at[g, way, 0])
+            for step in range(2):
+                y_copy(g, step, way).wait_send()
 
 
 def per_device(queries, resp_kv, prompt_kv, prompt_len, resp_len, dest, wo, residual):
@@ -347,19 +405,17 @@
     ny, tiles, half = dims.ny, dims.tiles, dims.half
     seg = heads * TL
 
-    slots = me * pdev + jnp.arange(pdev, dtype=jnp.int32)
-    every = jnp.arange(total, dtype=jnp.int32)
-    home = jnp.sum(jnp.where(dest[None, :] == slots[:, None], every[None, :], 0), axis=1) // pdev
-    scorer = lax.dynamic_slice(dest, (me * pdev,), (pdev,)) // pdev
-    live = lax.dynamic_slice(prompt_len, (me * pdev,), (pdev,))
-    here = jnp.arange(pdev, dtype=jnp.int32)
-    devices = jnp.arange(ndp, dtype=jnp.int32)
-    qidx = jnp.sum(jnp.where(home[None, :] == devices[:, None], here[None, :], 0), axis=1)
-    back = jnp.sum(jnp.where(scorer[None, :] == devices[:, None], here[None, :], 0), axis=1)
-    idx = jnp.concatenate([scorer, home, qidx, back, live]).astype(jnp.int32)
+    k = lax.broadcasted_iota(jnp.int32, (pdev + 2 * ndp, total), 0)
+    p = lax.broadcasted_iota(jnp.int32, (pdev + 2 * ndp, total), 1)
+    d = jnp.broadcast_to(dest[None, :], k.shape)
+    first, second = k < pdev, k < pdev + ndp
+    theirs = jnp.where(second, d, p) // pdev == me
+    same = jnp.where(first, d % pdev == k, jnp.where(second, p // pdev == k - pdev, d // pdev == k - pdev - ndp))
+    value = jnp.where(first, p // pdev, jnp.where(second, d, p) % pdev)
+    idx = jnp.sum(jnp.where(theirs & same, value, 0), axis=1)
 
     bf16, f32 = jnp.bfloat16, jnp.float32
-    layout = ["idx", "rlen", "q", "own", "kv_hbm", "wo_hbm", "res_hbm", "out"]
+    layout = ["idx", "dest", "live", "rlen", "q", "own", "kv_hbm", "wo_hbm", "res_hbm", "out"]
     scratch = []
 
     def add(name, shape):
@@ -368,6 +424,7 @@
 
     add("qv", pltpu.VMEM((pdev, dims.rows, HD), bf16))
     add("kv", pltpu.VMEM(prompt_kv.shape, bf16))
+    add("kt", pltpu.VMEM((pdev, HD, plen), bf16))
     add("wo", pltpu.VMEM((tiles, wo.shape[0], TN), bf16))
     add("res", pltpu.VMEM(residual.shape, bf16))
     add("fin", pltpu.VMEM(residual.shape, f32))
@@ -385,13 +442,15 @@
             add((name, g), pltpu.VMEM((ndp, 1, -(-n // 128) * 128), f32))
         for name in ("cs", "cr", "po"):
             add((name, g), pltpu.VMEM((tiles, ny, 2 * TL * size, TN), bf16))
-        for name in ("rs", "rr"):
-            add((name, g), pltpu.VMEM((2, ny - 1, half, 2 * TL * size, TN), bf16))
+        for name in ("xs", "xr"):
+            add((name, g), pltpu.VMEM((2, 2, half, 2 * TL * size, TN), bf16))
+        for name in ("ws", "wr"):
+            add((name, g), pltpu.VMEM((2, half, 2 * TL * size, TN), bf16))
     ng = len(GROUPS)
     add("load_sem", pltpu.SemaphoreType.DMA((2 + tiles,)))
     add("z_sem", pltpu.SemaphoreType.DMA((ng, 6)))
-    add("core_sem", pltpu.SemaphoreType.DMA((ng, 2)))
-    add("ring_sem", pltpu.SemaphoreType.DMA((ng, 2, ny - 1, 2)))
+    add("core_sem", pltpu.SemaphoreType.DMA((ng, 2, 2)))
+    add("ring_sem", pltpu.SemaphoreType.DMA((ng, 2, 2, 2)))
 
     smem = pl.BlockSpec(memory_space=pltpu.SMEM)
     vmem = pl.BlockSpec(memory_space=pltpu.VMEM)
@@ -399,13 +458,13 @@
     return pl.pallas_call(
         functools.partial(kernel, dims, layout),
         out_shape=jax.ShapeDtypeStruct(residual.shape, bf16),
-        in_specs=[smem, smem, vmem, vmem, hbm, hbm, hbm],
+        in_specs=[smem, smem, smem, smem, vmem, vmem, hbm, hbm, hbm],
         out_specs=vmem,
         scratch_shapes=scratch,
         compiler_params=pltpu.CompilerParams(
             collective_id=0, has_side_effects=True, vmem_limit_bytes=60 * 2**20
         ),
-    )(idx, resp_len, queries, resp_kv, prompt_kv, wo, residual)
+    )(idx, dest, prompt_len, resp_len.T, queries, resp_kv, prompt_kv, wo, residual)
 
 
 def solution(mesh):

time: 123 us -> 108 us (0.88)
  Pallas kernels: 116 us -> 102 us
  local copies, waits for them, and re-layouts: 5.2 us -> 2.46 us
  other arithmetic: 1.73 us -> 3.02 us
    pallas_call x1, Pallas kernels: 116 us -> 102 us  [per_device(): pl.pallas_call(functools.partial(kernel, dims, layout), out_shape=jax.Sha...]
    unnamed x2 -> x1, local copies, waits for them, and re-layouts: 3.82 us -> 2.46 us
where the time goes in v2:
time: 108 us
  Pallas kernels  102 us (94%)
  other arithmetic  3.02 us (3%)
  local copies, waits for them, and re-layouts  2.46 us (2%)
    pallas_call x1, Pallas kernels, per_device(): pl.pallas_call(functools.partial(kernel, dims, layout), out_shape=jax.Sha...  102 us
    unnamed x1, local copies, waits for them, and re-layouts  2.46 us

profile of v2, /device:TPU:2, one launch (start us, length us, event | category | flops | bytes accessed | tf_op | source)
XLA Modules:
  0.0 107.6 jit_solution(3539801754161241306)
XLA Ops:
  0.0 0.7 compare_and_fusion
  0.7 0.7 broadcast_add_fusion.2
  1.4 1.6 %fusion.1.refs_0_ = s32[80]{0:T(128)} fusion(s32[80]{0:T(128)S(1)} %get-tuple-element.14, s32[512]{0:T(512)S(1)} %get-tuple-element.10, s32[512]{0:T(512)S(1)} %get-tuple-element.8, s32[80]{0:T(128)S(1)} %get-tuple-element.15, s32[512]{0:T(512)S(1)} %get-tuple-element.11, s32[512]{0:T(512)S(1)} %get-tuple-element.12, s32[512]{0:T(512)S(1)} %get-tuple-element.9, ...), kind=kLoop, calls=%fused_computation.8 | loop fusion | flops 1351600 | bytes 16996 | tf_op jit(solution)/shard_map/reduce_sum | solution.py:415
  3.0 102.1 %shard_map.82 = bf16[80,8192]{1,0:T(8,128)(2,1)} custom-call(s32[80]{0:T(128)} %fusion.1.refs_0_, s32[512]{0:T(512)} %refs_1_.1, s32[512]{0:T(512)} %refs_2_.1, s32[5,16]{1,0:T(8,128)} %bitcast.1, bf16[640,512]{1,0:T(8,128)(2,1)} %refs_4_.1, bf16[640,256]{1,0:T(8,128)(2,1)} %refs_5_.1, bf16[16,512,256]{2,1,0:T(8,128)(2,1)} %refs_6_.1, ...), custom_call_target="tpu_custom_call" | custom-call | tf_op jit(solution)/shard_map/pallas_call | solution.py:458
  105.1 2.5 %copy.10 = bf16[80,8192]{1,0:T(8,128)(2,1)} copy(bf16[80,8192]{1,0:T(8,128)(2,1)} %shard_map.82) | data formatting | bytes 2621440
  (3 shorter events, 0.0 us)

commit v3 on v2

--- a/solution.py
+++ b/solution.py
@@ -12,7 +12,7 @@
 TL = 8
 GROUPS = ((0, 1), (1, 1), (2, 1), (3, 1), (4, 1))
 TN = 512
-SCOPES = False
+AHEAD = 2
 ATT_UNROLL = 4
 PROJ_UNROLL = 4
 MESH = pl.DeviceIdType.MESH
@@ -44,7 +44,7 @@
     idx, rlen, q_ref, own_ref = (names[k] for k in ("idx", "rlen", "q", "own"))
     dest, live = names["dest"], names["live"]
     kv_hbm, wo_hbm, res_hbm, out_ref = (names[k] for k in ("kv_hbm", "wo_hbm", "res_hbm", "out"))
-    qv, kv, kt, wo, res, fin = (names[k] for k in ("qv", "kv", "kt", "wo", "res", "fin"))
+    qv, kv, kt, vo, wo, res, fin = (names[k] for k in ("qv", "kv", "kt", "vo", "wo", "res", "fin"))
     orr, lser, ob, st_t, att = (names[k] for k in ("orr", "lser", "ob", "st_t", "att"))
     load_sem, z_sem, core_sem, ring_sem = (names[k] for k in ("load_sem", "z_sem", "core_sem", "ring_sem"))
     ndp, ny, pdev, heads = dims.ndp, dims.ny, dims.pdev, dims.heads
@@ -120,6 +120,8 @@
 
         def one(j, carry):
             kt[j] = jnp.transpose(kv[j, :, :HD])
+            vo[j, :, :HD] = jnp.ones((dims.plen, HD), bf16)
+            vo[j, :, HD:] = kv[j, :, HD:]
             return carry
 
         lax.fori_loop(0, pdev, one, 0, unroll=2)
@@ -166,9 +168,10 @@
             s = jnp.dot(qj, kt[j], preferred_element_type=f32)
             s = jnp.where(col < live[me * pdev + j], s * cc, NEG)
             m = jnp.max(s, axis=1, keepdims=True)
-            p = jnp.exp2(s - m)
-            l = jnp.sum(p, axis=1, keepdims=True)
-            o = jnp.dot(p.astype(bf16), kv[j, :, HD:], preferred_element_type=f32) / l
+            p = jnp.exp2(s - m).astype(bf16)
+            both = jnp.dot(p, vo[j], preferred_element_type=f32)
+            l, o = both[:, :HD], both[:, HD:]
+            o = o / l
             ob[j, pl.ds(0, n), :] = o.astype(bf16)
             return jnp.where(lane == j, m + jnp.log2(l), stat)
 
@@ -316,6 +319,19 @@
 
         lax.fori_loop(0, half, tile, 0, unroll=2)
 
+    def q_sent(g):
+        bulk_wait(names["qs", g].at[pl.ds(0, ndp - 1)], z_sem.at[g, 0])
+
+    def a_sent(g):
+        bulk_wait(names["as", g].at[pl.ds(0, ndp - 1)], z_sem.at[g, 2])
+        bulk_wait(names["ss", g].at[pl.ds(0, ndp - 1)], z_sem.at[g, 4])
+
+    def core_sent(g, way):
+        bulk_wait(names["cs", g].at[pl.ds(way * half, half)], core_sem.at[g, way, 0])
+
+    def y_sent(g, step, way):
+        y_copy(g, step, way).wait_send()
+
     def columns(body):
         def tile(n, carry):
             body(pl.ds(pl.multiple_of(n * TN, TN), TN))
@@ -340,16 +356,11 @@
         columns(start_total)
 
     def run(step, *args):
-        if SCOPES:
-            with jax.named_scope("_".join([step.__name__, *map(str, args)])):
-                step(*args)
-        else:
-            step(*args)
+        step(*args)
 
     run(all_here)
-    run(q_send, 0)
-    if ng > 1:
-        run(q_send, 1)
+    for g in range(min(AHEAD, ng)):
+        run(q_send, g)
     run(turn_keys)
     run(own_part)
     run(total_of_residual)
@@ -358,12 +369,8 @@
             run(q_wait, slot)
             run(attend, slot)
             run(a_send, slot)
-            if slot + 2 < ng:
-                run(q_send, slot + 2)
-        if 0 <= slot - 3:
-            for way in range(2):
-                run(y_wait, slot - 3, 1, way)
-                run(finish, slot - 3, way)
+            if slot + AHEAD < ng:
+                run(q_send, slot + AHEAD)
         if 0 <= slot - 1 < ng:
             run(a_wait, slot - 1)
             run(merge, slot - 1)
@@ -371,27 +378,29 @@
                 run(loaded)
             run(project, slot - 1, 0)
             run(project, slot - 1, 1)
+            for way in range(2):
+                run(core_wait, slot - 1, way)
+                run(y_first, slot - 1, way)
         if 0 <= slot - 2:
             for way in range(2):
                 run(y_wait, slot - 2, 0, way)
                 run(y_second, slot - 2, way)
-        if 0 <= slot - 1 < ng:
+        if 0 <= slot - 3:
             for way in range(2):
-                run(core_wait, slot - 1, way)
-                run(y_first, slot - 1, way)
+                run(y_wait, slot - 3, 1, way)
+                run(finish, slot - 3, way)
     for way in range(2):
         run(y_wait, ng - 1, 1, way)
         run(finish, ng - 1, way)
     columns(end_total)
 
     for g in range(ng):
-        bulk_wait(names["qs", g].at[pl.ds(0, ndp - 1)], z_sem.at[g, 0])
-        bulk_wait(names["as", g].at[pl.ds(0, ndp - 1)], z_sem.at[g, 2])
-        bulk_wait(names["ss", g].at[pl.ds(0, ndp - 1)], z_sem.at[g, 4])
+        run(q_sent, g)
+        run(a_sent, g)
         for way in range(2):
-            bulk_wait(names["cs", g].at[pl.ds(way * half, half)], core_sem.at[g, way, 0])
-            for step in range(2):
-                y_copy(g, step, way).wait_send()
+            run(core_sent, g, way)
+            run(y_sent, g, 0, way)
+            run(y_sent, g, 1, way)
 
 
 def per_device(queries, resp_kv, prompt_kv, prompt_len, resp_len, dest, wo, residual):
@@ -425,6 +434,7 @@
     add("qv", pltpu.VMEM((pdev, dims.rows, HD), bf16))
     add("kv", pltpu.VMEM(prompt_kv.shape, bf16))
     add("kt", pltpu.VMEM((pdev, HD, plen), bf16))
+    add("vo", pltpu.VMEM((pdev, plen, 2 * HD), bf16))
     add("wo", pltpu.VMEM((tiles, wo.shape[0], TN), bf16))
     add("res", pltpu.VMEM(residual.shape, bf16))
     add("fin", pltpu.VMEM(residual.shape, f32))

time: 108 us -> 104 us (0.963)
  Pallas kernels: 102 us -> 97.2 us
    pallas_call x1, Pallas kernels: 102 us -> 97.2 us  [per_device(): pl.pallas_call(functools.partial(kernel, dims, layout), out_shape=jax.Sha...]
where the time goes in v3:
time: 104 us; the launch traced here: 103 us
  Pallas kernels  97.2 us (93%)
  other arithmetic  3.02 us (3%)
  local copies, waits for them, and re-layouts  2.46 us (2%)
    pallas_call x1, Pallas kernels, per_device(): pl.pallas_call(functools.partial(kernel, dims, layout), out_shape=jax.Sha...  97.2 us
    unnamed x1, local copies, waits for them, and re-layouts  2.46 us

profile of v3, /device:TPU:2, one launch (start us, length us, event | category | flops | bytes accessed | tf_op | source)
XLA Modules:
  0.0 102.7 jit_solution(17996490473931862677)
XLA Ops:
  0.0 0.7 compare_and_fusion
  0.7 0.7 broadcast_add_fusion.2
  1.4 1.6 %fusion.1.refs_0_ = s32[80]{0:T(128)} fusion(s32[80]{0:T(128)S(1)} %get-tuple-element.14, s32[512]{0:T(512)S(1)} %get-tuple-element.10, s32[512]{0:T(512)S(1)} %get-tuple-element.8, s32[80]{0:T(128)S(1)} %get-tuple-element.15, s32[512]{0:T(512)S(1)} %get-tuple-element.11, s32[512]{0:T(512)S(1)} %get-tuple-element.12, s32[512]{0:T(512)S(1)} %get-tuple-element.9, ...), kind=kLoop, calls=%fused_computation.8 | loop fusion | flops 1351600 | bytes 16996 | tf_op jit(solution)/shard_map/reduce_sum | solution.py:424
  3.0 97.2 %shard_map.82 = bf16[80,8192]{1,0:T(8,128)(2,1)} custom-call(s32[80]{0:T(128)} %fusion.1.refs_0_, s32[512]{0:T(512)} %refs_1_.1, s32[512]{0:T(512)} %refs_2_.1, s32[5,16]{1,0:T(8,128)} %bitcast.1, bf16[640,512]{1,0:T(8,128)(2,1)} %refs_4_.1, bf16[640,256]{1,0:T(8,128)(2,1)} %refs_5_.1, bf16[16,512,256]{2,1,0:T(8,128)(2,1)} %refs_6_.1, ...), custom_call_target="tpu_custom_call" | custom-call | tf_op jit(solution)/shard_map/pallas_call | solution.py:468
  100.2 2.5 %copy.10 = bf16[80,8192]{1,0:T(8,128)(2,1)} copy(bf16[80,8192]{1,0:T(8,128)(2,1)} %shard_map.82) | data formatting | bytes 2621440
  (3 shorter events, 0.0 us)

commit v4 on v3

--- a/solution.py
+++ b/solution.py
@@ -2,6 +2,7 @@
 
 import jax
 import jax.numpy as jnp
+import numpy as np
 from jax import lax
 from jax.experimental import pallas as pl
 from jax.experimental.pallas import tpu as pltpu
@@ -13,7 +14,7 @@
 GROUPS = ((0, 1), (1, 1), (2, 1), (3, 1), (4, 1))
 TN = 512
 AHEAD = 2
-ATT_UNROLL = 4
+ATT_UNROLL = 8
 PROJ_UNROLL = 4
 MESH = pl.DeviceIdType.MESH
 LOG2E = 1.4426950408889634
@@ -414,13 +415,16 @@
     ny, tiles, half = dims.ny, dims.tiles, dims.half
     seg = heads * TL
 
-    k = lax.broadcasted_iota(jnp.int32, (pdev + 2 * ndp, total), 0)
-    p = lax.broadcasted_iota(jnp.int32, (pdev + 2 * ndp, total), 1)
-    d = jnp.broadcast_to(dest[None, :], k.shape)
+    k = np.arange(pdev + 2 * ndp, dtype=np.int32)[:, None]
+    p = np.arange(total, dtype=np.int32)[None, :]
     first, second = k < pdev, k < pdev + ndp
-    theirs = jnp.where(second, d, p) // pdev == me
-    same = jnp.where(first, d % pdev == k, jnp.where(second, p // pdev == k - pdev, d // pdev == k - pdev - ndp))
-    value = jnp.where(first, p // pdev, jnp.where(second, d, p) % pdev)
+    asked = np.where(first, k, np.where(second, k - pdev, k - pdev - ndp)).astype(np.int32)
+    p_dev, p_at = p // pdev, p % pdev
+    bits = (pdev - 1).bit_length()
+    d_dev, d_at = dest[None, :] >> bits, dest[None, :] & (pdev - 1)
+    theirs = jnp.where(second, d_dev, p_dev) == me
+    same = jnp.where(first, d_at, jnp.where(second, p_dev, d_dev)) == asked
+    value = jnp.where(first, p_dev, jnp.where(second, d_at, p_at))
     idx = jnp.sum(jnp.where(theirs & same, value, 0), axis=1)
 
     bf16, f32 = jnp.bfloat16, jnp.float32

time: 104 us -> 103 us (level)
  no operation moved by 1% of the time
where the time goes in v4:
time: 103 us; the launch traced here: 101 us
  Pallas kernels  96.5 us (94%)
  local copies, waits for them, and re-layouts  2.46 us (2%)
  other arithmetic  2.17 us (2%)
    pallas_call x1, Pallas kernels, per_device(): pl.pallas_call(functools.partial(kernel, dims, layout), out_shape=jax.Sha...  96.5 us
    unnamed x1, local copies, waits for them, and re-layouts  2.46 us

profile of v4, /device:TPU:2, one launch (start us, length us, event | category | flops | bytes accessed | tf_op | source)
XLA Modules:
  0.0 101.1 jit_solution(3566295249869484281)
XLA Ops:
  0.0 0.7 broadcast_shift-right-arithmetic_fusion
  0.7 1.5 %select_reduce_fusion.refs_0_ = s32[80]{0:T(128)} fusion(s32[512]{0:T(512)} %constant.34, s32[80]{0:T(128)} %constant.33, s32[512]{0:T(512)S(1)} %get-tuple-element.6, s32[]{:T(128)S(6)} %axis_index.15, s32[512]{0:T(512)} %constant.31, s32[512]{0:T(512)S(1)} %get-tuple-element.5, pred[80]{0:T(512)(128)(4,1)} %constant.32, pred[80]{0:T(512)(128)(4,1)} %constant.30), kind=kLoop, calls=%fused_computation | loop fusion | flops 409520 | bytes 8996 | tf_op jit(solution)/shard_map/reduce_sum | solution.py:428
  2.2 96.5 %shard_map.127 = bf16[80,8192]{1,0:T(8,128)(2,1)} custom-call(s32[80]{0:T(128)} %select_reduce_fusion.refs_0_, s32[512]{0:T(512)} %refs_1_.1, s32[512]{0:T(512)} %refs_2_.1, s32[5,16]{1,0:T(8,128)} %bitcast.1, bf16[640,512]{1,0:T(8,128)(2,1)} %refs_4_.1, bf16[640,256]{1,0:T(8,128)(2,1)} %refs_5_.1, bf16[16,512,256]{2,1,0:T(8,128)(2,1)} %refs_6_.1, ...), custom_call_target="tpu_custom_call" | custom-call | tf_op jit(solution)/shard_map/pallas_call | solution.py:472
  98.7 2.5 %copy.15 = bf16[80,8192]{1,0:T(8,128)(2,1)} copy(bf16[80,8192]{1,0:T(8,128)(2,1)} %shard_map.127) | data formatting | bytes 2621440
